TPU v7x, 256 devices: a whole 4x4x8 slice. The times are simulated.
256 devices in a mesh: leaf: 256 (over y, x, z, core).
Axes of the slice: x: 4, y: 4, z: 8, core: 2. Of those that a mesh axis runs over, the one named last changes fastest.
Arguments:
- points: float32 [28, 524288], P(None, 'leaf'), may hold values from -3 to 3
- tree_order: int32 [256, 2048], P('leaf'), may hold values from 0 to 2047, each once within a row
- leaf_basis: bfloat16 [1024, 512, 256], P('leaf'), may hold values from -0.25 to 0.25
- local_transfer: bfloat16 [1792, 256, 256], P('leaf'), may hold values from -0.2651875 to 0.2651875
- local_coupling: bfloat16 [768, 256, 256], P('leaf'), may hold values from -0.375 to 0.375
- device_transfer: bfloat16 [256, 6, 256, 256], P('leaf'), may hold values from -0.2651875 to 0.2651875, as said below
- device_coupling: bfloat16 [256, 8, 256, 256], P('leaf'), may hold values from -5.091169 to 5.091169, as said below
- solution: float32 [524288, 128], P('leaf'), may hold values from -6 to 6
- residual: float32 [524288, 128], P('leaf'), may hold values from -40 to 40
- direction: float32 [524288, 128], P('leaf'), may hold values from -40 to 40
Outputs:
- new_solution: float32 [524288, 128], P('leaf')
- new_residual: float32 [524288, 128], P('leaf')
- new_direction: float32 [524288, 128], P('leaf')
Inputs may be any that keep to these rules, and one draw needn't show every extreme that they name: `tree_order`: each row is a permutation of 0 to 2047. `device_transfer`: entry m - 1 of a device is the transfer matrix of its ancestor node that spans 2 ** m devices; every device under that node holds the same matrix. `device_coupling`: entry m of a device is the coupling matrix that multiplies the coefficients of the sibling of its ancestor spanning 2 ** m devices; the devices of the lower side hold B, those of the upper side its transpose.
All inputs are finite; a program needn't handle non-finite values.
Results may differ from a plain program's by a relative error of at most 0.035.
Values may be sent and summed in bfloat16 or wider, within the bound.
No kernel may reach another device: no remote copies, remote signals or barrier semaphores. Data moves between devices by JAX's collectives and lax.ppermute only.
A program may use at most 64 MiB of HBM per device.

v0:
```python
import jax
import jax.numpy as jnp
from jax import lax
from jax.sharding import PartitionSpec as P

ITERATIONS = 3


exact_mode = lax.Precision.HIGHEST
ridge_weight = 32.0
sharpness = 0.25


def swapped(array, axis, apart):
    return lax.ppermute(array, axis, [(i, i ^ 1 << apart) for i in range(lax.axis_size(axis))])


def rounded(value):
    return value.astype(jnp.bfloat16)


def to_parent(coeffs, blocks):
    return jnp.einsum("nij,nic->njc", blocks, coeffs, preferred_element_type=jnp.float32)


def to_child(coeffs, blocks):
    return jnp.einsum("nij,njc->nic", blocks, coeffs, preferred_element_type=jnp.float32)


def per_device(
    points,
    tree_order,
    leaf_basis,
    local_transfer,
    local_coupling,
    device_transfer,
    device_coupling,
    solution,
    residual,
    direction,
):
    leaves_here = leaf_basis.shape[0]
    leaf_rows = leaf_basis.shape[1]
    rank_size = leaf_basis.shape[2]
    columns = solution.shape[1]
    local_depth = leaves_here.bit_length() - 1
    device_depth = lax.axis_size("leaf").bit_length() - 1
    ordered = jnp.take(points, tree_order[0], axis=1)
    tree_points = ordered.reshape(ordered.shape[0], leaves_here, leaf_rows)
    squares = jnp.sum(tree_points * tree_points, axis=0)
    products = jnp.einsum(
        "fla,flb->lab",
        tree_points,
        tree_points,
        precision=exact_mode,
        preferred_element_type=jnp.float32,
    )
    kernels = rounded(
        jnp.exp(-sharpness * (squares[:, :, None] + squares[:, None, :] - 2.0 * products))
    )
    node_blocks = []
    offset = 0
    for height in range(local_depth + 1):
        number = leaves_here >> height
        node_blocks.append(local_transfer[offset : offset + number])
        offset += number
    pair_blocks = []
    offset = 0
    for height in range(local_depth):
        number = leaves_here >> height + 1
        pair_blocks.append(local_coupling[offset : offset + number])
        offset += number
    transfers = [node_blocks[local_depth][0]]
    for height in range(1, device_depth - 1):
        transfers.append(device_transfer[0, height - 1])
    norm_now = lax.psum(jnp.sum(residual * residual, axis=0), "leaf")
    for step_index in range(ITERATIONS):
        pieces = rounded(direction).reshape(leaves_here, leaf_rows, columns)
        upward = [
            rounded(
                jnp.einsum("lar,lac->lrc", leaf_basis, pieces, preferred_element_type=jnp.float32)
            )
        ]
        for apply_height in range(local_depth):
            term_block = rounded(to_parent(upward[apply_height], node_blocks[apply_height]))
            upward.append(
                rounded(term_block[0::2].astype(jnp.float32) + term_block[1::2].astype(jnp.float32))
            )
        sources = []
        for apply_height in range(local_depth):
            left_side = upward[apply_height][0::2]
            right_side = upward[apply_height][1::2]
            to_left = rounded(to_child(right_side, pair_blocks[apply_height]))
            to_right = rounded(to_parent(left_side, pair_blocks[apply_height]))
            sources.append(jnp.stack([to_left, to_right], axis=1).reshape(-1, rank_size, columns))
        current = upward[local_depth][0]
        across = []
        for apply_height in range(device_depth):
            coupling = device_coupling[0, apply_height]
            if apply_height + 1 < device_depth:
                term_block = rounded(
                    jnp.einsum(
                        "ij,ic->jc",
                        transfers[apply_height],
                        current,
                        preferred_element_type=jnp.float32,
                    )
                )
                other_coeffs, other_term = swapped((current, term_block), "leaf", apply_height)
                across.append(
                    rounded(
                        jnp.einsum(
                            "ij,jc->ic", coupling, other_coeffs, preferred_element_type=jnp.float32
                        )
                    )
                )
                current = rounded(term_block.astype(jnp.float32) + other_term.astype(jnp.float32))
            else:
                other_coeffs = swapped(current, "leaf", apply_height)
                across.append(
                    rounded(
                        jnp.einsum(
                            "ij,jc->ic", coupling, other_coeffs, preferred_element_type=jnp.float32
                        )
                    )
                )
        field_down = across[device_depth - 1]
        for apply_height in range(device_depth - 2, -1, -1):
            pushed = jnp.einsum(
                "ij,jc->ic", transfers[apply_height], field_down, preferred_element_type=jnp.float32
            )
            field_down = rounded(across[apply_height].astype(jnp.float32) + pushed)
        field_down = field_down[None]
        for apply_height in range(local_depth - 1, -1, -1):
            parent = jnp.repeat(field_down, 2, axis=0)
            field_down = rounded(
                sources[apply_height].astype(jnp.float32)
                + to_child(parent, node_blocks[apply_height])
            )
        near_part = jnp.einsum("lab,lbc->lac", kernels, pieces, preferred_element_type=jnp.float32)
        far_part = jnp.einsum(
            "lar,lrc->lac", leaf_basis, field_down, preferred_element_type=jnp.float32
        )
        applied = (near_part + far_part).reshape(-1, columns) + ridge_weight * direction
        curvature = lax.psum(jnp.sum(direction * applied, axis=0), "leaf")
        step_size = norm_now / curvature
        solution = solution + step_size * direction
        residual = residual - step_size * applied
        norm_next = lax.psum(jnp.sum(residual * residual, axis=0), "leaf")
        direction = residual + norm_next / norm_now * direction
        norm_now = norm_next
    return (solution, residual, direction)


def solution(mesh):
    placed = (
        P(None, "leaf"),
        P("leaf", None),
        P("leaf", None, None),
        P("leaf", None, None),
        P("leaf", None, None),
        P("leaf", None, None, None),
        P("leaf", None, None, None),
        P("leaf", None),
        P("leaf", None),
        P("leaf", None),
    )
    return jax.shard_map(
        per_device,
        mesh=mesh,
        in_specs=placed,
        out_specs=(P("leaf", None), P("leaf", None), P("leaf", None)),
        check_vma=False,
    )
```

profile of v0, /device:TPU:1, one launch (start us, length us, event | category | flops | bytes accessed | tf_op | source)
XLA Modules:
  0.0 718.9 jit_solution(18288288905137434442)
XLA Ops:
  3.9 3.2 collective-permute-start
  10.9 8.9 %gather_fusion = f32[2048,28]{1,0:T(8,128)} fusion(f32[28,2048]{0,1:T(8,128)} %copy.27, s32[2048]{0:T(1024)S(1)} %broadcast_clamp_fusion), kind=kCustom, calls=%fused_computation | custom fusion | bytes 466944 | tf_op jit(solution)/shard_map/jit(_take)/gather | solution.py:48
  24.4 4.4 exponential_convert_fusion
  29.8 3.0 collective-permute-start.5
  34.6 6.5 collective-permute-start.7
  49.0 3.1 collective-permute-start.11
  59.1 3.0 collective-permute-start.14
  64.5 5.7 collective-permute-start.6
  76.6 2.4 collective-permute-done.10
  89.0 3.2 fusion
  94.0 82.1 %all-reduce = (f32[128]{0:T(128)S(1)}, f32[128]{0:T(128)S(1)}) all-reduce(f32[128]{0:T(128)S(1)} %get-tuple-element.17, f32[128]{0:T(128)S(1)} %get-tuple-element.16), channel_id=1, replica_groups=mesh['leaf'=256] {'leaf'}, use_global_device_ids=true, to_apply=%region_1.2 | all-reduce | flops 256 | bytes 2048 | tf_op jit(solution)/shard_map/psum | solution.py:76
  176.2 2.7 multiply_reduce_fusion.4
  178.9 73.2 %psum.51 = f32[128]{0:T(128)S(1)} all-reduce(f32[128]{0:T(128)S(1)} %get-tuple-element.13), channel_id=1, replica_groups=mesh['leaf'=256] {'leaf'}, use_global_device_ids=true, to_apply=%region_6.7 | all-reduce | flops 128 | bytes 1024 | tf_op jit(solution)/shard_map/psum | solution.py:149
  252.1 2.4 fusion.367
  270.9 3.3 collective-permute-start.22
  274.4 3.6 collective-permute-done.22
  279.4 4.9 collective-permute-start.15
  286.0 2.5 collective-permute-start.26
  323.3 3.2 fusion.1
  328.3 82.4 %psum.52 = f32[128]{0:T(128)S(1)} all-reduce(f32[128]{0:T(128)S(1)} %multiply_reduce_fusion.3), channel_id=1, replica_groups=mesh['leaf'=256] {'leaf'}, use_global_device_ids=true, to_apply=%region_8.9 | all-reduce | flops 128 | bytes 1024 | tf_op jit(solution)/shard_map/psum | solution.py:145
  410.8 3.0 multiply_reduce_fusion.2
  413.8 72.7 %psum.53 = f32[128]{0:T(128)S(1)} all-reduce(f32[128]{0:T(128)S(1)} %get-tuple-element.9), channel_id=1, replica_groups=mesh['leaf'=256] {'leaf'}, use_global_device_ids=true, to_apply=%region_10.11 | all-reduce | flops 128 | bytes 1024 | tf_op jit(solution)/shard_map/psum | solution.py:149
  486.5 2.8 fusion.366
  500.6 2.7 collective-permute-start.37
  503.4 4.2 collective-permute-done.37
  508.8 3.9 collective-permute-start.30
  514.1 2.4 collective-permute-start.41
  529.3 2.8 collective-permute-start.36
  555.8 82.6 %psum.54 = f32[128]{0:T(128)S(1)} all-reduce(f32[128]{0:T(128)S(1)} %multiply_reduce_fusion.1), channel_id=1, replica_groups=mesh['leaf'=256] {'leaf'}, use_global_device_ids=true, to_apply=%region_12.13 | all-reduce | flops 128 | bytes 1024 | tf_op jit(solution)/shard_map/psum | solution.py:145
  638.3 3.9 multiply_reduce_fusion
  642.3 73.5 %psum.55 = f32[128]{0:T(128)S(1)} all-reduce(f32[128]{0:T(128)S(1)} %get-tuple-element.5), channel_id=1, replica_groups=mesh['leaf'=256] {'leaf'}, use_global_device_ids=true, to_apply=%region_14.15 | all-reduce | flops 128 | bytes 1024 | tf_op jit(solution)/shard_map/psum | solution.py:149
  715.8 2.6 multiply_add_fusion
  (265 shorter events, 155.7 us)
Async XLA Ops:
  3.9 83.5 %collective-permute-start = (bf16[256,128]{0,1:T(8,128)(2,1)}, bf16[256,128]{0,1:T(8,128)(2,1)}, u32[]{:S(2)}, u32[]{:S(2)}) collective-permute-start(bf16[256,128]{0,1:T(8,128)(2,1)} %fusion.311), channel_id=1, source_target_pairs={{0,1},{1,0},{2,3},{3,2},{4,5},{5,4},{6,7},{7,6},{8,9},{9,8},{10,11... | collective-permute-start | bytes 196616 | tf_op jit(solution)/shard_map/ppermute | solution.py:15
  8.1 15.1 %collective-permute-start.1 = (bf16[256,128]{0,1:T(8,128)(2,1)S(1)}, bf16[256,128]{0,1:T(8,128)(2,1)}, u32[]{:S(2)}, u32[]{:S(2)}) collective-permute-start(bf16[256,128]{0,1:T(8,128)(2,1)S(1)} %fusion.93), channel_id=1, source_target_pairs={{0,1},{1,0},{2,3},{3,2},{4,5},{5,4},{6,7},{7,6},{8,9},{9,8},{10,11... | collective-permute-start | bytes 196616 | tf_op jit(solution)/shard_map/ppermute | solution.py:15
  24.3 4.6 collective-permute-start.3
  29.8 4.6 collective-permute-start.5
  34.6 8.2 %collective-permute-start.7 = (bf16[256,128]{0,1:T(8,128)(2,1)S(1)}, bf16[256,128]{0,1:T(8,128)(2,1)S(1)}, u32[]{:S(2)}, u32[]{:S(2)}) collective-permute-start(bf16[256,128]{0,1:T(8,128)(2,1)S(1)} %fusion.96), channel_id=1, source_target_pairs={{0,8},{1,9},{2,10},{3,11},{4,12},{5,13},{6,14},{7,15},{8,0},{9,1},... | collective-permute-start | bytes 196616 | tf_op jit(solution)/shard_map/ppermute | solution.py:15
  49.0 5.9 collective-permute-start.11
  59.1 11.1 %collective-permute-start.14 = (bf16[256,128]{0,1:T(8,128)(2,1)S(1)}, bf16[256,128]{0,1:T(8,128)(2,1)S(1)}, u32[]{:S(2)}, u32[]{:S(2)}) collective-permute-start(bf16[256,128]{0,1:T(8,128)(2,1)S(1)} %add_convert_fusion.19), channel_id=1, source_target_pairs={{0,128},{1,129},{2,130},{3,131},{4,132},{5,133},{6,134},{7,135},{8... | collective-permute-start | bytes 196616 | tf_op jit(solution)/shard_map/ppermute | solution.py:15
  63.0 23.1 %collective-permute-start.2 = (bf16[256,128]{0,1:T(8,128)(2,1)}, bf16[256,128]{0,1:T(8,128)(2,1)}, u32[]{:S(2)}, u32[]{:S(2)}) collective-permute-start(bf16[256,128]{0,1:T(8,128)(2,1)} %copy-done.13), channel_id=1, source_target_pairs={{0,2},{1,3},{2,0},{3,1},{4,6},{5,7},{6,4},{7,5},{8,10},{9,11},{10,... | collective-permute-start | bytes 196616 | tf_op jit(solution)/shard_map/ppermute | solution.py:15
  63.0 21.8 %collective-permute-start.4 = (bf16[256,128]{0,1:T(8,128)(2,1)}, bf16[256,128]{0,1:T(8,128)(2,1)}, u32[]{:S(2)}, u32[]{:S(2)}) collective-permute-start(bf16[256,128]{0,1:T(8,128)(2,1)} %copy-done.15), channel_id=1, source_target_pairs={{0,4},{1,5},{2,6},{3,7},{4,0},{5,1},{6,2},{7,3},{8,12},{9,13},{10,... | collective-permute-start | bytes 196616 | tf_op jit(solution)/shard_map/ppermute | solution.py:15
  64.5 19.0 %collective-permute-start.6 = (bf16[256,128]{0,1:T(8,128)(2,1)S(1)}, bf16[256,128]{0,1:T(8,128)(2,1)}, u32[]{:S(2)}, u32[]{:S(2)}) collective-permute-start(bf16[256,128]{0,1:T(8,128)(2,1)S(1)} %copy-done.18), channel_id=1, source_target_pairs={{0,8},{1,9},{2,10},{3,11},{4,12},{5,13},{6,14},{7,15},{8,0},{9,1},... | collective-permute-start | bytes 196616 | tf_op jit(solution)/shard_map/ppermute | solution.py:15
  73.7 5.2 collective-permute-start.10
  265.1 4.1 collective-permute-start.20
  270.9 7.1 collective-permute-start.22
  278.7 5.7 collective-permute-start.24
  279.4 39.8 %collective-permute-start.15 = (bf16[256,128]{0,1:T(8,128)(2,1)}, bf16[256,128]{0,1:T(8,128)(2,1)}, u32[]{:S(2)}, u32[]{:S(2)}) collective-permute-start(bf16[256,128]{0,1:T(8,128)(2,1)} %fusion.312), channel_id=1, source_target_pairs={{0,1},{1,0},{2,3},{3,2},{4,5},{5,4},{6,7},{7,6},{8,9},{9,8},{10,11... | collective-permute-start | bytes 196616 | tf_op jit(solution)/shard_map/ppermute | solution.py:15
  286.0 5.4 collective-permute-start.26
  295.6 6.2 collective-permute-start.29
  297.6 20.3 %collective-permute-start.17 = (bf16[256,128]{0,1:T(8,128)(2,1)}, bf16[256,128]{0,1:T(8,128)(2,1)}, u32[]{:S(2)}, u32[]{:S(2)}) collective-permute-start(bf16[256,128]{0,1:T(8,128)(2,1)} %add_convert_fusion.17), channel_id=1, source_target_pairs={{0,2},{1,3},{2,0},{3,1},{4,6},{5,7},{6,4},{7,5},{8,10},{9,11},{10,... | collective-permute-start | bytes 196616 | tf_op jit(solution)/shard_map/ppermute | solution.py:15
  297.9 18.8 %collective-permute-start.19 = (bf16[256,128]{0,1:T(8,128)(2,1)}, bf16[256,128]{0,1:T(8,128)(2,1)}, u32[]{:S(2)}, u32[]{:S(2)}) collective-permute-start(bf16[256,128]{0,1:T(8,128)(2,1)} %add_convert_fusion.16), channel_id=1, source_target_pairs={{0,4},{1,5},{2,6},{3,7},{4,0},{5,1},{6,2},{7,3},{8,12},{9,13},{10,... | collective-permute-start | bytes 196616 | tf_op jit(solution)/shard_map/ppermute | solution.py:15
  299.4 15.9 %collective-permute-start.21 = (bf16[256,128]{0,1:T(8,128)(2,1)}, bf16[256,128]{0,1:T(8,128)(2,1)}, u32[]{:S(2)}, u32[]{:S(2)}) collective-permute-start(bf16[256,128]{0,1:T(8,128)(2,1)} %add_convert_fusion.15), channel_id=1, source_target_pairs={{0,8},{1,9},{2,10},{3,11},{4,12},{5,13},{6,14},{7,15},{8,0},{9,1},... | collective-permute-start | bytes 196616 | tf_op jit(solution)/shard_map/ppermute | solution.py:15
  305.6 4.9 collective-permute-start.25
  492.2 3.9 collective-permute-start.33
  496.3 4.1 collective-permute-start.35
  500.6 7.1 collective-permute-start.37
  507.9 4.7 collective-permute-start.39
  508.8 40.8 %collective-permute-start.30 = (bf16[256,128]{0,1:T(8,128)(2,1)S(1)}, bf16[256,128]{0,1:T(8,128)(2,1)}, u32[]{:S(2)}, u32[]{:S(2)}) collective-permute-start(bf16[256,128]{0,1:T(8,128)(2,1)S(1)} %fusion.313), channel_id=1, source_target_pairs={{0,1},{1,0},{2,3},{3,2},{4,5},{5,4},{6,7},{7,6},{8,9},{9,8},{10,11... | collective-permute-start | bytes 196616 | tf_op jit(solution)/shard_map/ppermute | solution.py:15
  514.1 5.3 collective-permute-start.41
  525.1 7.0 collective-permute-start.44
  527.0 21.2 %collective-permute-start.32 = (bf16[256,128]{0,1:T(8,128)(2,1)S(1)}, bf16[256,128]{0,1:T(8,128)(2,1)S(1)}, u32[]{:S(2)}, u32[]{:S(2)}) collective-permute-start(bf16[256,128]{0,1:T(8,128)(2,1)S(1)} %add_convert_fusion.9), channel_id=1, source_target_pairs={{0,2},{1,3},{2,0},{3,1},{4,6},{5,7},{6,4},{7,5},{8,10},{9,11},{10,... | collective-permute-start | bytes 196616 | tf_op jit(solution)/shard_map/ppermute | solution.py:15
  529.3 17.7 %collective-permute-start.34 = (bf16[256,128]{0,1:T(8,128)(2,1)}, bf16[256,128]{0,1:T(8,128)(2,1)S(1)}, u32[]{:S(2)}, u32[]{:S(2)}) collective-permute-start(bf16[256,128]{0,1:T(8,128)(2,1)} %copy-done.14), channel_id=1, source_target_pairs={{0,4},{1,5},{2,6},{3,7},{4,0},{5,1},{6,2},{7,3},{8,12},{9,13},{10,... | collective-permute-start | bytes 196616 | tf_op jit(solution)/shard_map/ppermute | solution.py:15
  529.3 16.5 %collective-permute-start.36 = (bf16[256,128]{0,1:T(8,128)(2,1)}, bf16[256,128]{0,1:T(8,128)(2,1)S(1)}, u32[]{:S(2)}, u32[]{:S(2)}) collective-permute-start(bf16[256,128]{0,1:T(8,128)(2,1)} %copy-done.16), channel_id=1, source_target_pairs={{0,8},{1,9},{2,10},{3,11},{4,12},{5,13},{6,14},{7,15},{8,0},{9,1},... | collective-permute-start | bytes 196616 | tf_op jit(solution)/shard_map/ppermute | solution.py:15
  536.2 4.8 collective-permute-start.40
  (42 other events, 235.9 us)
where the time goes:
time: 729 us; the launch traced here: 719 us
  blocking collectives  467 us (64%)
  starting transfers between devices  76 us (10%)
  matrix products  70.1 us (10%)
  waiting for transfers between devices  42.6 us (6%)
  other arithmetic  38.1 us (5%)
  local copies, waits for them, and re-layouts  23.5 us (3%)
    psum x3, blocking collectives, per_device(): norm_next = lax.psum(jnp.sum(residual * residual, axis=0), 'leaf')  219 us
    psum x2, blocking collectives, per_device(): curvature = lax.psum(jnp.sum(direction * applied, axis=0), 'leaf')  165 us
    psum x1, blocking collectives, per_device(): norm_now = lax.psum(jnp.sum(residual * residual, axis=0), 'leaf')  82.1 us
    ppermute x45, starting transfers between devices, swapped(): lax.ppermute(array, axis, [(i, i ^ 1 << apart) for i in range(lax.axis_si...  76 us
    ppermute x45, waiting for transfers between devices, swapped(): lax.ppermute(array, axis, [(i, i ^ 1 << apart) for i in range(lax.axis_si...  42.6 us
    dot_general x21, matrix products, per_device(): jnp.einsum('ij,jc->ic', transfers[apply_height], field_down, preferred_el...  26.7 us
  transfers between devices with their start and end apart: 45, of which 22 were waited for; matrix products, arithmetic and copies ran while one was open for 11% of the time, Pallas kernels for 0%

commit v1 on v0

v1 whole, which is shorter than its diff:
```python
import functools

import jax
import jax.numpy as jnp
from jax import lax
from jax.experimental import pallas as pl
from jax.experimental.pallas import tpu as pltpu
from jax.sharding import PartitionSpec as P

ITERATIONS = 3
ridge_weight = 32.0
sharpness = 0.25
LEAVES = 4
ROWS = 512
RANK = 256
COLS = 128
LEVELS = 8
PAYLOAD = RANK + 32
BF = jnp.bfloat16
F32 = jnp.float32


def dot(left, right):
    return jnp.dot(left, right, preferred_element_type=F32)


def params(size=48 << 20):
    return pltpu.CompilerParams(vmem_limit_bytes=size)


def whole(shape):
    return pl.BlockSpec(shape, lambda *_: (0,) * len(shape))


def partners(count):
    turn = {0: 6, 1: 7, 2: 4, 3: 5, 4: 2, 5: 3, 6: 0, 7: 1}
    levels = []
    for level in range(count.bit_length() - 1):
        pairs = []
        for i in range(count):
            if level == 3:
                j = i & ~14 | turn[i >> 1 & 7] << 1
            elif level in (5, 7):
                j = i ^ 3 << level - 1
            else:
                j = i ^ 1 << level
            pairs.append((i, j))
        levels.append(pairs)
    return levels


def split3(value):
    high = value.astype(BF)
    rest = value - high.astype(F32)
    mid = rest.astype(BF)
    low = (rest - mid.astype(F32)).astype(BF)
    return high, mid, low


def pack_sums(sums):
    high, mid, low = split3(sums)
    parts = [piece.astype(F32) for piece in (high, mid, low)] + [jnp.zeros((8, COLS), F32)]
    return jnp.concatenate(parts, axis=0).astype(BF)


def unpack_sums(packed):
    wide = packed.astype(F32)
    return wide[0:8] + wide[8:16] + wide[16:24]


def row_of(sums, index):
    return sums[index : index + 1]


def stack_rows(*rows):
    place = lax.broadcasted_iota(jnp.int32, (8, COLS), 0)
    total = jnp.zeros((8, COLS), F32)
    for index, row in enumerate(rows):
        total = total + jnp.where(place == index, row, 0.0)
    return total


def leaf_kernel(points_ref, order_ref, out_ref, pieces):
    @pl.when(pl.program_id(0) == 0)
    def _():
        value = points_ref[...]
        high, mid, low = split3(value)
        gap = jnp.zeros((4, value.shape[1]), F32)
        pieces[...] = jnp.concatenate(
            [high.astype(F32), gap, mid.astype(F32), gap, low.astype(F32), gap], axis=0
        ).astype(BF)

    total = pieces.shape[1]
    place = lax.broadcasted_iota(jnp.int32, (total, ROWS), 0)
    chosen = jnp.where(place == order_ref[0], 1.0, 0.0).astype(BF)
    moved = dot(pieces[...], chosen)
    high, mid, low = moved[0:32], moved[32:64], moved[64:96]
    full = high + mid + low
    half = -0.5 * jnp.sum(full * full, axis=0, keepdims=True)
    h3, m3, l3 = (piece.astype(F32) for piece in split3(half))
    one = jnp.ones_like(half)
    place8 = lax.broadcasted_iota(jnp.int32, (8, ROWS), 0)

    def rows8(*rows):
        block = jnp.zeros((8, ROWS), F32)
        for index, row in enumerate(rows):
            block = block + jnp.where(place8 == index, row, 0.0)
        return block

    pad = jnp.zeros((8, ROWS), F32)
    left = jnp.concatenate(
        [high, high, mid, high, low, mid, rows8(h3, m3, l3, one, one, one), pad], axis=0
    ).astype(BF)
    right = jnp.concatenate(
        [high, mid, high, low, high, mid, rows8(one, one, one, h3, m3, l3), pad], axis=0
    ).astype(BF)
    inner = lax.dot_general(
        left, right, (((0,), (0,)), ((), ())), preferred_element_type=F32
    )
    out_ref[0] = jnp.exp((2.0 * sharpness) * inner).astype(BF)


def make_kernels(points, order):
    features, total = points.shape
    return pl.pallas_call(
        leaf_kernel,
        grid=(LEAVES,),
        in_specs=[
            whole((features, total)),
            pl.BlockSpec((1, 1, ROWS), lambda i: (i, 0, 0)),
        ],
        out_specs=pl.BlockSpec((1, ROWS, ROWS), lambda i: (i, 0, 0)),
        out_shape=jax.ShapeDtypeStruct((LEAVES, ROWS, ROWS), BF),
        scratch_shapes=[pltpu.VMEM((96, total), BF)],
        compiler_params=params(),
        cost_estimate=pl.CostEstimate(
            flops=2 * LEAVES * (96 * total + 208 * ROWS) * ROWS,
            bytes_accessed=4 << 20,
            transcendentals=LEAVES * ROWS * ROWS,
        ),
        name="leaf_kernels",
    )(points, order.reshape(LEAVES, 1, ROWS))


def compose_kernel(basis, local_r, local_b, device_r, device_b, other_r, wide, tall, mix, up, down):
    first = [local_r[i] for i in range(LEAVES)]
    second = [local_r[LEAVES], local_r[LEAVES + 1]]
    for i in range(LEAVES):
        path = dot(first[i], second[i // 2]).astype(BF)
        reach = dot(basis[i], path).astype(BF)
        wide[i, :, :RANK] = reach
        wide[i, :, RANK:] = basis[i]
        tall[i, :RANK, :] = reach.T
        tall[i, RANK:, :] = basis[i].T
    flipped = [block.T for block in first]
    pair = local_b[2]
    across = [pair, pair.T]
    for i in range(LEAVES):
        side = dot(first[i], across[i // 2]).astype(BF)
        for j in range(LEAVES):
            if i == j:
                block = jnp.zeros((RANK, RANK), BF)
            elif i // 2 == j // 2:
                block = local_b[i // 2]
                if i % 2:
                    block = block.T
            else:
                block = dot(side, flipped[j]).astype(BF)
            mix[i * RANK : (i + 1) * RANK, j * RANK : (j + 1) * RANK] = block
    path = None
    for level in range(LEVELS):
        coupling = device_b[0, level]
        down[level, :RANK, :] = coupling
        if path is None:
            down[level, RANK:, :] = coupling
        else:
            down[level, RANK:, :] = dot(path, coupling).astype(BF)
        if level + 1 < LEVELS:
            step = local_r[LEAVES + 2] if level == 0 else device_r[0, level - 1]
            up[level, :, :RANK] = step.T
            up[level, :, RANK:] = other_r[level].T
            path = step if path is None else dot(path, step).astype(BF)


def compose(basis, local_r, local_b, device_r, device_b, other_r):
    shapes = [
        (LEAVES, ROWS, 2 * RANK),
        (LEAVES, 2 * RANK, ROWS),
        (LEAVES * RANK, LEAVES * RANK),
        (LEVELS - 1, RANK, 2 * RANK),
        (LEVELS, 2 * RANK, RANK),
    ]

    def entry(basis, local_r, local_b, device_r, device_b, *rest):
        others = [ref[...] for ref in rest[: LEVELS - 1]]
        compose_kernel(
            basis, local_r, local_b, device_r, device_b, others, *rest[LEVELS - 1 :]
        )

    operands = [basis, local_r, local_b, device_r, device_b] + list(other_r)
    return pl.pallas_call(
        entry,
        in_specs=[pl.BlockSpec(memory_space=pltpu.VMEM)] * len(operands),
        out_specs=[pl.BlockSpec(memory_space=pltpu.VMEM)] * len(shapes),
        out_shape=[jax.ShapeDtypeStruct(shape, BF) for shape in shapes],
        compiler_params=params(),
        name="compose",
    )(*operands)


def climb_kernel(own, got, up, down, *rest):
    if len(rest) == 3:
        field_in, out, field_out = rest
    else:
        out, field_out = rest
        field_in = None
    mine = own[:RANK]
    theirs = got[:RANK]
    moved = dot(up[0, :, :RANK], mine) + dot(up[0, :, RANK:], theirs)
    out[:RANK] = moved.astype(BF)
    felt = dot(down[0], theirs)
    energy = jnp.sum(mine.astype(F32) * felt[:RANK], axis=0, keepdims=True)
    zero = jnp.zeros_like(energy)
    sums = unpack_sums(own[RANK:]) + unpack_sums(got[RANK:])
    out[RANK:] = pack_sums(sums + stack_rows(zero, 2.0 * energy))
    if field_in is None:
        field_out[...] = felt[RANK:]
    else:
        field_out[...] = field_in[...] + felt[RANK:]


def climb(level, own, got, up, down, field):
    operands = [own, got, up, down] + ([] if field is None else [field])
    specs = [
        whole((PAYLOAD, COLS)),
        whole((PAYLOAD, COLS)),
        pl.BlockSpec((1, RANK, 2 * RANK), lambda i: (level, 0, 0)),
        pl.BlockSpec((1, 2 * RANK, RANK), lambda i: (level, 0, 0)),
    ] + ([] if field is None else [whole((RANK, COLS))])
    return pl.pallas_call(
        climb_kernel,
        grid=(1,),
        in_specs=specs,
        out_specs=[whole((PAYLOAD, COLS)), whole((RANK, COLS))],
        out_shape=[
            jax.ShapeDtypeStruct((PAYLOAD, COLS), BF),
            jax.ShapeDtypeStruct((RANK, COLS), F32),
        ],
        compiler_params=params(8 << 20),
        name="climb",
    )(*operands)


def finish_sweep(own, got, down, field_in, scalars_in, first, field, scalars):
    mine = own[:RANK]
    theirs = got[:RANK]
    felt = dot(down[0], theirs)
    field[...] = (field_in[...] + felt[RANK:]).astype(BF)
    energy = jnp.sum(mine.astype(F32) * felt[:RANK], axis=0, keepdims=True)
    sums = unpack_sums(own[RANK:]) + unpack_sums(got[RANK:])
    norm = row_of(sums, 0)
    curve = row_of(sums, 1) + 2.0 * energy
    if first:
        scalars[...] = stack_rows(norm, curve, norm / curve)
    else:
        turn = norm / scalars_in[0:1]
        bend = curve + turn * (2.0 * row_of(sums, 2) + turn * scalars_in[1:2])
        scalars[...] = stack_rows(norm, bend, norm / bend, turn)


def leaf_update(first, wide, base, near, residual, direction, image, solved, field, scalars):
    reach = wide[0]
    applied = base[...] + dot(reach[:, :RANK], field[...]) + dot(reach[:, RANK:], near[0])
    size = scalars[2:3]
    if first:
        step = direction[...]
        pushed = applied
    else:
        turn = scalars[3:4]
        step = residual[...] + turn * direction[...]
        pushed = applied + turn * image[...]
    return step, pushed, solved[...] + size * step, residual[...] - size * pushed


def leaf_apply(vector, kernel, tall, base, gathered, total, i):
    low = vector.astype(BF)
    out = dot(kernel[0], low) + ridge_weight * vector
    base[...] = out
    coeffs = dot(tall[0], low)
    gathered[i] = coeffs[RANK:].astype(BF)

    @pl.when(i == 0)
    def _():
        total[...] = coeffs[:RANK]

    @pl.when(i > 0)
    def _():
        total[...] += coeffs[:RANK]

    return out


def column_sum(value):
    return jnp.sum(value, axis=0, keepdims=True)


def add_sums(sums, i, rows):
    @pl.when(i == 0)
    def _():
        sums[...] = rows

    @pl.when(i > 0)
    def _():
        sums[...] += rows


def close_leaves(mix, gathered, total, sums, near, payload):
    packed = gathered[...].reshape(LEAVES * RANK, COLS)
    felt = dot(mix[...], packed)
    energy = column_sum(packed.astype(F32) * felt)
    near[...] = felt.astype(BF).reshape(LEAVES, RANK, COLS)
    payload[:RANK] = total[...].astype(BF)
    payload[RANK:] = pack_sums(sums[...] + stack_rows(jnp.zeros_like(energy), energy))


def begin_kernel(
    residual, direction, kernel, tall, mix, base, near, payload, gathered, total, sums
):
    i = pl.program_id(0)
    vector = direction[...]
    out = leaf_apply(vector, kernel, tall, base, gathered, total, i)
    here = residual[...]
    add_sums(sums, i, stack_rows(column_sum(here * here), column_sum(vector * out)))

    @pl.when(i == LEAVES - 1)
    def _():
        close_leaves(mix, gathered, total, sums, near, payload)


def turn_kernel(
    first,
    own,
    got,
    down,
    field_in,
    scalars_in,
    wide,
    base_in,
    near_in,
    residual,
    direction,
    image,
    solved,
    kernel,
    tall,
    mix,
    residual_out,
    direction_out,
    image_out,
    solved_out,
    base,
    near,
    payload,
    scalars,
    gathered,
    total,
    sums,
    field,
):
    i = pl.program_id(0)

    @pl.when(i == 0)
    def _():
        finish_sweep(own, got, down, field_in, scalars_in, first, field, scalars)

    step, pushed, solved_new, here = leaf_update(
        first, wide, base_in, near_in, residual, direction, image, solved, field, scalars
    )
    residual_out[...] = here
    direction_out[...] = step
    image_out[...] = pushed
    solved_out[...] = solved_new
    out = leaf_apply(here, kernel, tall, base, gathered, total, i)
    add_sums(
        sums,
        i,
        stack_rows(column_sum(here * here), column_sum(here * out), column_sum(here * pushed)),
    )

    @pl.when(i == LEAVES - 1)
    def _():
        close_leaves(mix, gathered, total, sums, near, payload)


def end_kernel(
    own,
    got,
    down,
    field_in,
    scalars_in,
    wide,
    base_in,
    near_in,
    residual,
    direction,
    image,
    solved,
    residual_out,
    direction_out,
    solved_out,
    scalars,
    sums,
    field,
):
    i = pl.program_id(0)

    @pl.when(i == 0)
    def _():
        finish_sweep(own, got, down, field_in, scalars_in, False, field, scalars)

    step, pushed, solved_new, here = leaf_update(
        False, wide, base_in, near_in, residual, direction, image, solved, field, scalars
    )
    residual_out[...] = here
    direction_out[...] = step
    solved_out[...] = solved_new
    add_sums(sums, i, stack_rows(column_sum(here * here)))


rows_spec = pl.BlockSpec((ROWS, COLS), lambda i: (i, 0))
kernel_spec = pl.BlockSpec((1, ROWS, ROWS), lambda i: (i, 0, 0))
wide_spec = pl.BlockSpec((1, ROWS, 2 * RANK), lambda i: (i, 0, 0))
tall_spec = pl.BlockSpec((1, 2 * RANK, ROWS), lambda i: (i, 0, 0))
mix_spec = whole((LEAVES * RANK, LEAVES * RANK))
near_spec = pl.BlockSpec((1, RANK, COLS), lambda i: (i, 0, 0))
near_whole = whole((LEAVES, RANK, COLS))
payload_spec = whole((PAYLOAD, COLS))
small_spec = whole((8, COLS))
field_spec = whole((RANK, COLS))
last_spec = pl.BlockSpec((1, 2 * RANK, RANK), lambda i: (LEVELS - 1, 0, 0))

vector_shape = jax.ShapeDtypeStruct((LEAVES * ROWS, COLS), F32)
near_shape = jax.ShapeDtypeStruct((LEAVES, RANK, COLS), BF)
payload_shape = jax.ShapeDtypeStruct((PAYLOAD, COLS), BF)
small_shape = jax.ShapeDtypeStruct((8, COLS), F32)


def leaf_scratch():
    return [
        pltpu.VMEM((LEAVES, RANK, COLS), BF),
        pltpu.VMEM((RANK, COLS), F32),
        pltpu.VMEM((8, COLS), F32),
    ]


def begin(residual, direction, kernels, tall, mix):
    return pl.pallas_call(
        begin_kernel,
        grid=(LEAVES,),
        in_specs=[rows_spec, rows_spec, kernel_spec, tall_spec, mix_spec],
        out_specs=[rows_spec, near_whole, payload_spec],
        out_shape=[vector_shape, near_shape, payload_shape],
        scratch_shapes=leaf_scratch(),
        compiler_params=params(),
        name="begin",
    )(residual, direction, kernels, tall, mix)


def turn(first, own, got, down, field, scalars, wide, base, near, vectors, kernels, tall, mix):
    return pl.pallas_call(
        functools.partial(turn_kernel, first),
        grid=(LEAVES,),
        in_specs=[
            payload_spec,
            payload_spec,
            last_spec,
            field_spec,
            small_spec,
            wide_spec,
            rows_spec,
            near_spec,
        ]
        + [rows_spec] * 4
        + [kernel_spec, tall_spec, mix_spec],
        out_specs=[rows_spec] * 5 + [near_whole, payload_spec, small_spec],
        out_shape=[vector_shape] * 5 + [near_shape, payload_shape, small_shape],
        scratch_shapes=leaf_scratch() + [pltpu.VMEM((RANK, COLS), BF)],
        compiler_params=params(),
        name="turn",
    )(own, got, down, field, scalars, wide, base, near, *vectors, kernels, tall, mix)


def end(own, got, down, field, scalars, wide, base, near, vectors):
    return pl.pallas_call(
        end_kernel,
        grid=(LEAVES,),
        in_specs=[
            payload_spec,
            payload_spec,
            last_spec,
            field_spec,
            small_spec,
            wide_spec,
            rows_spec,
            near_spec,
        ]
        + [rows_spec] * 4,
        out_specs=[rows_spec] * 3 + [small_spec, small_spec],
        out_shape=[vector_shape] * 3 + [small_shape, small_shape],
        scratch_shapes=[pltpu.VMEM((RANK, COLS), BF)],
        compiler_params=params(),
        name="end",
    )(own, got, down, field, scalars, wide, base, near, *vectors)


def per_device(
    count,
    points,
    tree_order,
    leaf_basis,
    local_transfer,
    local_coupling,
    device_transfer,
    device_coupling,
    solution,
    residual,
    direction,
):
    routes = partners(count)
    other = []
    for level in range(LEVELS - 1):
        matrix = local_transfer[6] if level == 0 else device_transfer[0, level - 1]
        other.append(lax.ppermute(matrix, "leaf", routes[level]))
    kernels = make_kernels(points, tree_order)
    wide, tall, mix, up, down = compose(
        leaf_basis, local_transfer, local_coupling, device_transfer, device_coupling, other
    )
    base, near, payload = begin(residual, direction, kernels, tall, mix)
    image = direction
    scalars = jnp.ones((8, COLS), F32)
    for step in range(ITERATIONS):
        field = None
        for level in range(LEVELS - 1):
            got = lax.ppermute(payload, "leaf", routes[level])
            payload, field = climb(level, payload, got, up, down, field)
        got = lax.ppermute(payload, "leaf", routes[LEVELS - 1])
        vectors = (residual, direction, image, solution)
        if step + 1 < ITERATIONS:
            residual, direction, image, solution, base, near, payload, scalars = turn(
                step == 0,
                payload,
                got,
                down,
                field,
                scalars,
                wide,
                base,
                near,
                vectors,
                kernels,
                tall,
                mix,
            )
        else:
            residual, direction, solution, scalars, sums = end(
                payload, got, down, field, scalars, wide, base, near, vectors
            )
    spread = jnp.broadcast_to(sums[0:1], (count, COLS))
    parts = lax.all_to_all(spread, "leaf", 0, 0, tiled=True)
    norm = jnp.sum(parts, axis=0, keepdims=True)
    direction = residual + norm / scalars[0:1] * direction
    return (solution, residual, direction)


def solution(mesh):
    placed = (
        P(None, "leaf"),
        P("leaf", None),
        P("leaf", None, None),
        P("leaf", None, None),
        P("leaf", None, None),
        P("leaf", None, None, None),
        P("leaf", None, None, None),
        P("leaf", None),
        P("leaf", None),
        P("leaf", None),
    )
    return jax.shard_map(
        functools.partial(per_device, mesh.shape["leaf"]),
        mesh=mesh,
        in_specs=placed,
        out_specs=(P("leaf", None), P("leaf", None), P("leaf", None)),
        check_vma=False,
    )
```

time: 729 us -> 202 us (0.28); the launches traced: 719 us -> 202 us
  blocking collectives: 467 us -> 26 us
  matrix products: 70.1 us -> 0 us
  Pallas kernels: 0 us -> 42.7 us
  other arithmetic: 38.1 us -> 2.36 us
  waiting for transfers between devices: 42.6 us -> 73.1 us
  starting transfers between devices: 76 us -> 52.9 us
  local copies, waits for them, and re-layouts: 23.5 us -> 3.99 us
    psum x6 -> x0, blocking collectives: 467 us -> none  [the longest x3 219 us: per_device(): norm_next = lax.psum(jnp.sum(residual * residual, axis=0), 'leaf')]
    dot_general x76 -> x0, matrix products: 70.1 us -> none  [the longest x21 26.7 us: per_device(): jnp.einsum('ij,jc->ic', transfers[apply_height], field_down, preferred_el...]
    pallas_call x0 -> x27, Pallas kernels: none -> 42.7 us  [the longest x2 16.6 us: turn(): pl.pallas_call(functools.partial(turn_kernel, first), grid=(LEAVES,), in_...]
    ppermute x45 -> x31, waiting for transfers between devices: 42.6 us -> 73.1 us  [the longest x21 63.3 us: per_device(): got = lax.ppermute(payload, 'leaf', routes[level])]
    all_to_all x0 -> x1, blocking collectives: none -> 26 us  [per_device(): parts = lax.all_to_all(spread, 'leaf', 0, 0, tiled=True)]
    ppermute x45 -> x31, starting transfers between devices: 76 us -> 52.9 us  [the longest x21 33.6 us: per_device(): got = lax.ppermute(payload, 'leaf', routes[level])]
    convert_element_type x30 -> x0, other arithmetic: 16.7 us -> none  [the longest x27 14.2 us: rounded(): return value.astype(jnp.bfloat16)]
    reduce_sum x7 -> x1, other arithmetic: 16.7 us -> 0.05 us  [per_device(): norm = jnp.sum(parts, axis=0, keepdims=True)]
  transfers between devices with their start and end apart: 45 -> 31, of which waited for: 22 -> 25; matrix products, arithmetic and copies ran while one was open for 11% -> 1% of each run, Pallas kernels for 0% -> 2%
where the time goes in v1:
time: 202 us
  waiting for transfers between devices  73.1 us (36%)
  starting transfers between devices  52.9 us (26%)
  Pallas kernels  42.7 us (21%)
  blocking collectives  26 us (13%)
  local copies, waits for them, and re-layouts  3.99 us (2%)
  other arithmetic  2.36 us (1%)
    ppermute x21, waiting for transfers between devices, per_device(): got = lax.ppermute(payload, 'leaf', routes[level])  63.3 us
    ppermute x21, starting transfers between devices, per_device(): got = lax.ppermute(payload, 'leaf', routes[level])  33.6 us
    all_to_all x1, blocking collectives, per_device(): parts = lax.all_to_all(spread, 'leaf', 0, 0, tiled=True)  26 us
    pallas_call x2, Pallas kernels, turn(): pl.pallas_call(functools.partial(turn_kernel, first), grid=(LEAVES,), in_...  16.6 us
    ppermute x7, starting transfers between devices, per_device(): other.append(lax.ppermute(matrix, 'leaf', routes[level]))  13.4 us
    ppermute x3, waiting for transfers between devices, per_device(): got = lax.ppermute(payload, 'leaf', routes[LEVELS - 1])  7.54 us
    pallas_call x21, Pallas kernels, climb(): pl.pallas_call(climb_kernel, grid=(1,), in_specs=specs, out_specs=[whole(...  6.37 us
    pallas_call x1, Pallas kernels, compose(): pl.pallas_call(entry, in_specs=[pl.BlockSpec(memory_space=pltpu.VMEM)] *...  6.12 us
  transfers between devices with their start and end apart: 31, of which 25 were waited for; matrix products, arithmetic and copies ran while one was open for 1% of the time, Pallas kernels for 2%

profile of v1, /device:TPU:1, one launch (start us, length us, event | category | flops | bytes accessed | tf_op | source)
XLA Modules:
  0.0 202.0 jit_solution(12354032021276153001)
XLA Ops:
  1.5 3.3 %collective-permute-start = (bf16[256,256]{1,0:T(8,128)(2,1)S(1)}, bf16[256,256]{1,0:T(8,128)(2,1)S(1)}, u32[]{:S(2)}, u32[]{:S(2)}) collective-permute-start(bf16[256,256]{1,0:T(8,128)(2,1)S(1)} %slice_bitcast_fusion.6), channel_id=1, source_target_pairs={{0,1},{1,0},{2,3},{3,2},{4,5},{5,4},{6,7},{7,6},{8,9},{9,8},{10,11... | collective-permute-start | bytes 393224 | tf_op jit(solution)/shard_map/ppermute | solution.py:533
  8.3 6.0 %collective-permute-start.3 = (bf16[256,256]{1,0:T(8,128)(2,1)S(1)}, bf16[256,256]{1,0:T(8,128)(2,1)S(1)}, u32[]{:S(2)}, u32[]{:S(2)}) collective-permute-start(bf16[256,256]{1,0:T(8,128)(2,1)S(1)} %get-tuple-element.148), channel_id=1, source_target_pairs={{0,12},{1,13},{2,14},{3,15},{4,8},{5,9},{6,10},{7,11},{8,4},{9,5},... | collective-permute-start | bytes 393224 | tf_op jit(solution)/shard_map/ppermute | solution.py:533
  17.9 3.5 %leaf_kernels.1.kernel = bf16[4,512,512]{2,1,0:T(8,128)(2,1)S(1)} custom-call(f32[28,2048]{1,0:T(8,128)S(1)} %copy-done.19, s32[4,1,512]{2,1,0:T(1,128)S(1)} %bitcast.24), custom_call_target="tpu_custom_call" | custom-call | flops 1241513984 | bytes 4194304 | tf_op jit(solution)/shard_map/leaf_kernels/pallas_call | solution.py:125
  21.4 2.2 %collective-permute-done.1.rest_1_ = bf16[256,256]{1,0:T(8,128)(2,1)S(1)} collective-permute-done((bf16[256,256]{1,0:T(8,128)(2,1)S(1)}, bf16[256,256]{1,0:T(8,128)(2,1)S(1)}, u32[]{:S(2)}, u32[]{:S(2)}) %collective-permute-start.1) | collective-permute-done | bytes 131104 | tf_op jit(solution)/shard_map/ppermute | solution.py:533
  23.6 6.1 %compose.1 = (bf16[4,512,512]{2,1,0:T(8,128)(2,1)}, bf16[4,512,512]{2,1,0:T(8,128)(2,1)}, bf16[1024,1024]{1,0:T(8,128)(2,1)}, bf16[7,256,512]{2,1,0:T(8,128)(2,1)}, bf16[8,512,256]{2,1,0:T(8,128)(2,1)}) custom-call(bf16[4,512,256]{2,1,0:T(8,128)(2,1)S(1)} %copy-done.9, bf16[7,256,256]{2,1,0:T(8,128)(2,1)S(1)} %copy-done.8, ...), custom_call_target="tpu_custom_call" | custom-call | tf_op jit(solution)/shard_map/compose/pallas_call | solution.py:201
  29.8 5.3 %begin.1 = (f32[2048,128]{1,0:T(8,128)S(1)}, bf16[4,256,128]{2,1,0:T(8,128)(2,1)S(1)}, bf16[288,128]{1,0:T(8,128)(2,1)S(1)}) custom-call(f32[2048,128]{1,0:T(8,128)S(1)} %copy-done.6, f32[2048,128]{1,0:T(8,128)S(1)} %copy-done.5, bf16[4,512,512]{2,1,0:T(8,128)(2,1)S(1)} %leaf_kernels.1.kernel, bf16[4,512,512]{2,1,0:T(8,128)(2,1)} %get-tuple-element.74.tall, ...), custom_call_target="tpu_custom_call" | custom-call | tf_op jit(solution)/shard_map/begin/pallas_call | solution.py:457
  43.2 2.6 %collective-permute-done.9.got = bf16[288,128]{1,0:T(8,128)(2,1)S(1)} collective-permute-done((bf16[288,128]{1,0:T(8,128)(2,1)S(1)}, bf16[288,128]{1,0:T(8,128)(2,1)S(1)}, u32[]{:S(2)}, u32[]{:S(2)}) %collective-permute-start.9) | collective-permute-done | bytes 73760 | tf_op jit(solution)/shard_map/ppermute | solution.py:544
  47.6 3.9 %collective-permute-done.10.got = bf16[288,128]{1,0:T(8,128)(2,1)S(1)} collective-permute-done((bf16[288,128]{1,0:T(8,128)(2,1)S(1)}, bf16[288,128]{1,0:T(8,128)(2,1)S(1)}, u32[]{:S(2)}, u32[]{:S(2)}) %collective-permute-start.10) | collective-permute-done | bytes 73760 | tf_op jit(solution)/shard_map/ppermute | solution.py:544
  56.5 3.6 %collective-permute-done.12.got = bf16[288,128]{1,0:T(8,128)(2,1)S(1)} collective-permute-done((bf16[288,128]{1,0:T(8,128)(2,1)S(1)}, bf16[288,128]{1,0:T(8,128)(2,1)S(1)}, u32[]{:S(2)}, u32[]{:S(2)}) %collective-permute-start.12) | collective-permute-done | bytes 73760 | tf_op jit(solution)/shard_map/ppermute | solution.py:544
  60.7 3.0 %collective-permute-done.13.got = bf16[288,128]{1,0:T(8,128)(2,1)S(1)} collective-permute-done((bf16[288,128]{1,0:T(8,128)(2,1)S(1)}, bf16[288,128]{1,0:T(8,128)(2,1)S(1)}, u32[]{:S(2)}, u32[]{:S(2)}) %collective-permute-start.13) | collective-permute-done | bytes 73760 | tf_op jit(solution)/shard_map/ppermute | solution.py:544
  66.0 2.5 %collective-permute-done.14.got = bf16[288,128]{1,0:T(8,128)(2,1)S(1)} collective-permute-done((bf16[288,128]{1,0:T(8,128)(2,1)S(1)}, bf16[288,128]{1,0:T(8,128)(2,1)S(1)}, u32[]{:S(2)}, u32[]{:S(2)}) %collective-permute-start.14) | collective-permute-done | bytes 73760 | tf_op jit(solution)/shard_map/ppermute | solution.py:546
  68.5 8.3 %turn.2 = (f32[2048,128]{1,0:T(8,128)S(1)}, f32[2048,128]{1,0:T(8,128)S(1)}, f32[2048,128]{1,0:T(8,128)S(1)}, f32[2048,128]{1,0:T(8,128)S(1)}, f32[2048,128]{1,0...) custom-call(bf16[288,128]{1,0:T(8,128)(2,1)S(1)} %get-tuple-element.91.own, ...), custom_call_target="tpu_custom_call" | custom-call | tf_op jit(solution)/shard_map/turn/pallas_call | solution.py:470
  76.9 8.5 %collective-permute-start.15 = (bf16[288,128]{1,0:T(8,128)(2,1)S(1)}, bf16[288,128]{1,0:T(8,128)(2,1)S(1)}, u32[]{:S(2)}, u32[]{:S(2)}) collective-permute-start(bf16[288,128]{1,0:T(8,128)(2,1)S(1)} %get-tuple-element.96.own), channel_id=1, source_target_pairs={{0,1},{1,0},{2,3},{3,2},{4,5},{5,4},{6,7},{7,6},{8,9},{9,8},{10,11... | collective-permute-start | bytes 221192 | tf_op jit(solution)/shard_map/ppermute | solution.py:544
  88.6 2.4 %collective-permute-done.16.got = bf16[288,128]{1,0:T(8,128)(2,1)S(1)} collective-permute-done((bf16[288,128]{1,0:T(8,128)(2,1)S(1)}, bf16[288,128]{1,0:T(8,128)(2,1)S(1)}, u32[]{:S(2)}, u32[]{:S(2)}) %collective-permute-start.16) | collective-permute-done | bytes 73760 | tf_op jit(solution)/shard_map/ppermute | solution.py:544
  92.6 4.1 %collective-permute-done.17.got = bf16[288,128]{1,0:T(8,128)(2,1)S(1)} collective-permute-done((bf16[288,128]{1,0:T(8,128)(2,1)S(1)}, bf16[288,128]{1,0:T(8,128)(2,1)S(1)}, u32[]{:S(2)}, u32[]{:S(2)}) %collective-permute-start.17) | collective-permute-done | bytes 73760 | tf_op jit(solution)/shard_map/ppermute | solution.py:544
  97.1 5.3 %collective-permute-done.18.got = bf16[288,128]{1,0:T(8,128)(2,1)S(1)} collective-permute-done((bf16[288,128]{1,0:T(8,128)(2,1)S(1)}, bf16[288,128]{1,0:T(8,128)(2,1)S(1)}, u32[]{:S(2)}, u32[]{:S(2)}) %collective-permute-start.18) | collective-permute-done | bytes 73760 | tf_op jit(solution)/shard_map/ppermute | solution.py:544
  103.0 3.0 %collective-permute-done.19.got = bf16[288,128]{1,0:T(8,128)(2,1)S(1)} collective-permute-done((bf16[288,128]{1,0:T(8,128)(2,1)S(1)}, bf16[288,128]{1,0:T(8,128)(2,1)S(1)}, u32[]{:S(2)}, u32[]{:S(2)}) %collective-permute-start.19) | collective-permute-done | bytes 73760 | tf_op jit(solution)/shard_map/ppermute | solution.py:544
  107.1 3.6 %collective-permute-done.20.got = bf16[288,128]{1,0:T(8,128)(2,1)S(1)} collective-permute-done((bf16[288,128]{1,0:T(8,128)(2,1)S(1)}, bf16[288,128]{1,0:T(8,128)(2,1)S(1)}, u32[]{:S(2)}, u32[]{:S(2)}) %collective-permute-start.20) | collective-permute-done | bytes 73760 | tf_op jit(solution)/shard_map/ppermute | solution.py:544
  111.2 3.5 %collective-permute-done.21.got = bf16[288,128]{1,0:T(8,128)(2,1)S(1)} collective-permute-done((bf16[288,128]{1,0:T(8,128)(2,1)S(1)}, bf16[288,128]{1,0:T(8,128)(2,1)S(1)}, u32[]{:S(2)}, u32[]{:S(2)}) %collective-permute-start.21) | collective-permute-done | bytes 73760 | tf_op jit(solution)/shard_map/ppermute | solution.py:544
  116.9 2.5 %collective-permute-done.22.got = bf16[288,128]{1,0:T(8,128)(2,1)S(1)} collective-permute-done((bf16[288,128]{1,0:T(8,128)(2,1)S(1)}, bf16[288,128]{1,0:T(8,128)(2,1)S(1)}, u32[]{:S(2)}, u32[]{:S(2)}) %collective-permute-start.22) | collective-permute-done | bytes 73760 | tf_op jit(solution)/shard_map/ppermute | solution.py:546
  119.5 8.3 %turn.3 = (f32[2048,128]{1,0:T(8,128)S(1)}, f32[2048,128]{1,0:T(8,128)S(1)}, f32[2048,128]{1,0:T(8,128)S(1)}, f32[2048,128]{1,0:T(8,128)S(1)}, f32[2048,128]{1,0...) custom-call(bf16[288,128]{1,0:T(8,128)(2,1)S(1)} %get-tuple-element.109.own, ...), custom_call_target="tpu_custom_call" | custom-call | tf_op jit(solution)/shard_map/turn/pallas_call | solution.py:470
  127.8 6.7 %collective-permute-start.23 = (bf16[288,128]{1,0:T(8,128)(2,1)S(1)}, bf16[288,128]{1,0:T(8,128)(2,1)S(1)}, u32[]{:S(2)}, u32[]{:S(2)}) collective-permute-start(bf16[288,128]{1,0:T(8,128)(2,1)S(1)} %get-tuple-element.118.own), channel_id=1, source_target_pairs={{0,1},{1,0},{2,3},{3,2},{4,5},{5,4},{6,7},{7,6},{8,9},{9,8},{10,11... | collective-permute-start | bytes 221192 | tf_op jit(solution)/shard_map/ppermute | solution.py:544
  137.7 2.4 %collective-permute-done.24.got = bf16[288,128]{1,0:T(8,128)(2,1)S(1)} collective-permute-done((bf16[288,128]{1,0:T(8,128)(2,1)S(1)}, bf16[288,128]{1,0:T(8,128)(2,1)S(1)}, u32[]{:S(2)}, u32[]{:S(2)}) %collective-permute-start.24) | collective-permute-done | bytes 73760 | tf_op jit(solution)/shard_map/ppermute | solution.py:544
  141.8 4.1 %collective-permute-done.25.got = bf16[288,128]{1,0:T(8,128)(2,1)S(1)} collective-permute-done((bf16[288,128]{1,0:T(8,128)(2,1)S(1)}, bf16[288,128]{1,0:T(8,128)(2,1)S(1)}, u32[]{:S(2)}, u32[]{:S(2)}) %collective-permute-start.25) | collective-permute-done | bytes 73760 | tf_op jit(solution)/shard_map/ppermute | solution.py:544
  146.4 5.3 %collective-permute-done.26.got = bf16[288,128]{1,0:T(8,128)(2,1)S(1)} collective-permute-done((bf16[288,128]{1,0:T(8,128)(2,1)S(1)}, bf16[288,128]{1,0:T(8,128)(2,1)S(1)}, u32[]{:S(2)}, u32[]{:S(2)}) %collective-permute-start.26) | collective-permute-done | bytes 73760 | tf_op jit(solution)/shard_map/ppermute | solution.py:544
  152.0 3.2 %collective-permute-done.27.got = bf16[288,128]{1,0:T(8,128)(2,1)S(1)} collective-permute-done((bf16[288,128]{1,0:T(8,128)(2,1)S(1)}, bf16[288,128]{1,0:T(8,128)(2,1)S(1)}, u32[]{:S(2)}, u32[]{:S(2)}) %collective-permute-start.27) | collective-permute-done | bytes 73760 | tf_op jit(solution)/shard_map/ppermute | solution.py:544
  156.4 3.6 %collective-permute-done.28.got = bf16[288,128]{1,0:T(8,128)(2,1)S(1)} collective-permute-done((bf16[288,128]{1,0:T(8,128)(2,1)S(1)}, bf16[288,128]{1,0:T(8,128)(2,1)S(1)}, u32[]{:S(2)}, u32[]{:S(2)}) %collective-permute-start.28) | collective-permute-done | bytes 73760 | tf_op jit(solution)/shard_map/ppermute | solution.py:544
  160.4 3.5 %collective-permute-done.29.got = bf16[288,128]{1,0:T(8,128)(2,1)S(1)} collective-permute-done((bf16[288,128]{1,0:T(8,128)(2,1)S(1)}, bf16[288,128]{1,0:T(8,128)(2,1)S(1)}, u32[]{:S(2)}, u32[]{:S(2)}) %collective-permute-start.29) | collective-permute-done | bytes 73760 | tf_op jit(solution)/shard_map/ppermute | solution.py:544
  166.2 2.5 %collective-permute-done.30.got = bf16[288,128]{1,0:T(8,128)(2,1)S(1)} collective-permute-done((bf16[288,128]{1,0:T(8,128)(2,1)S(1)}, bf16[288,128]{1,0:T(8,128)(2,1)S(1)}, u32[]{:S(2)}, u32[]{:S(2)}) %collective-permute-start.30) | collective-permute-done | bytes 73760 | tf_op jit(solution)/shard_map/ppermute | solution.py:546
  168.7 4.9 %end.1 = (f32[2048,128]{1,0:T(8,128)}, f32[2048,128]{1,0:T(8,128)S(1)}, f32[2048,128]{1,0:T(8,128)}, f32[8,128]{1,0:T(8,128)S(1)}, f32[8,128]{1,0:T(8,128)S(1)}) custom-call(bf16[288,128]{1,0:T(8,128)(2,1)S(1)} %get-tuple-element.131.own, bf16[288,128]{1,0:T(8,128)(2,1)S(1)} %collective-permute-done.30.got, bf16[8,512,256]{2,1,0:T(8,128)(2,1)} %get-tuple-element.78.down, ...), custom_call_target="tpu_custom_call" | custom-call | tf_op jit(solution)/shard_map/end/pallas_call | solution.py:494
  173.7 26.0 %all_to_all.6 = f32[256,1,128]{2,1,0:T(1,128)S(1)} all-to-all(f32[256,1,128]{2,1,0:T(1,128)S(1)} %broadcast_in_dim.12), channel_id=1, replica_groups=mesh['leaf'=256] {'leaf'}, dimensions={0} | all-to-all | bytes 262144 | tf_op jit(solution)/shard_map/all_to_all | solution.py:569
  199.7 2.3 %multiply_add_fusion = f32[2048,128]{1,0:T(8,128)} fusion(f32[2048,128]{1,0:T(8,128)} %get-tuple-element.72, f32[2048,128]{1,0:T(8,128)S(1)} %get-tuple-element.144, f32[128]{0:T(128)S(1)} %fusion), kind=kLoop, calls=%fused_computation | loop fusion | flops 524288 | bytes 3146240 | tf_op jit(solution)/shard_map/add | solution.py:571
  (108 shorter events, 45.2 us)
Async XLA Ops:
  1.5 12.7 %collective-permute-start = (bf16[256,256]{1,0:T(8,128)(2,1)S(1)}, bf16[256,256]{1,0:T(8,128)(2,1)S(1)}, u32[]{:S(2)}, u32[]{:S(2)}) collective-permute-start(bf16[256,256]{1,0:T(8,128)(2,1)S(1)} %slice_bitcast_fusion.6), channel_id=1, source_target_pairs={{0,1},{1,0},{2,3},{3,2},{4,5},{5,4},{6,7},{7,6},{8,9},{9,8},{10,11... | collective-permute-start | bytes 393224 | tf_op jit(solution)/shard_map/ppermute | solution.py:533
  6.1 9.3 %collective-permute-start.6 = (bf16[256,256]{1,0:T(8,128)(2,1)S(1)}, bf16[256,256]{1,0:T(8,128)(2,1)S(1)}, u32[]{:S(2)}, u32[]{:S(2)}) collective-permute-start(bf16[256,256]{1,0:T(8,128)(2,1)S(1)} %get-tuple-element.145), channel_id=1, source_target_pairs={{0,64},{1,65},{2,66},{3,67},{4,68},{5,69},{6,70},{7,71},{8,72},{9,... | collective-permute-start | bytes 393224 | tf_op jit(solution)/shard_map/ppermute | solution.py:533
  6.2 15.2 %collective-permute-start.5 = (bf16[256,256]{1,0:T(8,128)(2,1)S(1)}, bf16[256,256]{1,0:T(8,128)(2,1)S(1)}, u32[]{:S(2)}, u32[]{:S(2)}) collective-permute-start(bf16[256,256]{1,0:T(8,128)(2,1)S(1)} %get-tuple-element.146), channel_id=1, source_target_pairs={{0,48},{1,49},{2,50},{3,51},{4,52},{5,53},{6,54},{7,55},{8,56},{9,... | collective-permute-start | bytes 393224 | tf_op jit(solution)/shard_map/ppermute | solution.py:533
  8.3 13.1 %collective-permute-start.4 = (bf16[256,256]{1,0:T(8,128)(2,1)S(1)}, bf16[256,256]{1,0:T(8,128)(2,1)S(1)}, u32[]{:S(2)}, u32[]{:S(2)}) collective-permute-start(bf16[256,256]{1,0:T(8,128)(2,1)S(1)} %get-tuple-element.147), channel_id=1, source_target_pairs={{0,16},{1,17},{2,18},{3,19},{4,20},{5,21},{6,22},{7,23},{8,24},{9,... | collective-permute-start | bytes 393224 | tf_op jit(solution)/shard_map/ppermute | solution.py:533
  8.3 13.1 %collective-permute-start.3 = (bf16[256,256]{1,0:T(8,128)(2,1)S(1)}, bf16[256,256]{1,0:T(8,128)(2,1)S(1)}, u32[]{:S(2)}, u32[]{:S(2)}) collective-permute-start(bf16[256,256]{1,0:T(8,128)(2,1)S(1)} %get-tuple-element.148), channel_id=1, source_target_pairs={{0,12},{1,13},{2,14},{3,15},{4,8},{5,9},{6,10},{7,11},{8,4},{9,5},... | collective-permute-start | bytes 393224 | tf_op jit(solution)/shard_map/ppermute | solution.py:533
  14.3 7.1 %collective-permute-start.2 = (bf16[256,256]{1,0:T(8,128)(2,1)S(1)}, bf16[256,256]{1,0:T(8,128)(2,1)S(1)}, u32[]{:S(2)}, u32[]{:S(2)}) collective-permute-start(bf16[256,256]{1,0:T(8,128)(2,1)S(1)} %get-tuple-element.149), channel_id=1, source_target_pairs={{0,4},{1,5},{2,6},{3,7},{4,0},{5,1},{6,2},{7,3},{8,12},{9,13},{10,... | collective-permute-start | bytes 393224 | tf_op jit(solution)/shard_map/ppermute | solution.py:533
  15.5 8.1 %collective-permute-start.1 = (bf16[256,256]{1,0:T(8,128)(2,1)S(1)}, bf16[256,256]{1,0:T(8,128)(2,1)S(1)}, u32[]{:S(2)}, u32[]{:S(2)}) collective-permute-start(bf16[256,256]{1,0:T(8,128)(2,1)S(1)} %get-tuple-element.150), channel_id=1, source_target_pairs={{0,2},{1,3},{2,0},{3,1},{4,6},{5,7},{6,4},{7,5},{8,10},{9,11},{10,... | collective-permute-start | bytes 393224 | tf_op jit(solution)/shard_map/ppermute | solution.py:533
  35.2 2.5 %collective-permute-start.7 = (bf16[288,128]{1,0:T(8,128)(2,1)S(1)}, bf16[288,128]{1,0:T(8,128)(2,1)S(1)}, u32[]{:S(2)}, u32[]{:S(2)}) collective-permute-start(bf16[288,128]{1,0:T(8,128)(2,1)S(1)} %get-tuple-element.76.own), channel_id=1, source_target_pairs={{0,1},{1,0},{2,3},{3,2},{4,5},{5,4},{6,7},{7,6},{8,9},{9,8},{10,11... | collective-permute-start | bytes 221192 | tf_op jit(solution)/shard_map/ppermute | solution.py:544
  38.0 3.3 %collective-permute-start.8 = (bf16[288,128]{1,0:T(8,128)(2,1)S(1)}, bf16[288,128]{1,0:T(8,128)(2,1)S(1)}, u32[]{:S(2)}, u32[]{:S(2)}) collective-permute-start(bf16[288,128]{1,0:T(8,128)(2,1)S(1)} %get-tuple-element.79.own), channel_id=1, source_target_pairs={{0,2},{1,3},{2,0},{3,1},{4,6},{5,7},{6,4},{7,5},{8,10},{9,11},{10,... | collective-permute-start | bytes 221192 | tf_op jit(solution)/shard_map/ppermute | solution.py:544
  41.6 4.2 %collective-permute-start.9 = (bf16[288,128]{1,0:T(8,128)(2,1)S(1)}, bf16[288,128]{1,0:T(8,128)(2,1)S(1)}, u32[]{:S(2)}, u32[]{:S(2)}) collective-permute-start(bf16[288,128]{1,0:T(8,128)(2,1)S(1)} %get-tuple-element.81.own), channel_id=1, source_target_pairs={{0,4},{1,5},{2,6},{3,7},{4,0},{5,1},{6,2},{7,3},{8,12},{9,13},{10,... | collective-permute-start | bytes 221192 | tf_op jit(solution)/shard_map/ppermute | solution.py:544
  46.1 5.5 %collective-permute-start.10 = (bf16[288,128]{1,0:T(8,128)(2,1)S(1)}, bf16[288,128]{1,0:T(8,128)(2,1)S(1)}, u32[]{:S(2)}, u32[]{:S(2)}) collective-permute-start(bf16[288,128]{1,0:T(8,128)(2,1)S(1)} %get-tuple-element.83.own), channel_id=1, source_target_pairs={{0,12},{1,13},{2,14},{3,15},{4,8},{5,9},{6,10},{7,11},{8,4},{9,5},... | collective-permute-start | bytes 221192 | tf_op jit(solution)/shard_map/ppermute | solution.py:544
  51.9 3.3 %collective-permute-start.11 = (bf16[288,128]{1,0:T(8,128)(2,1)S(1)}, bf16[288,128]{1,0:T(8,128)(2,1)S(1)}, u32[]{:S(2)}, u32[]{:S(2)}) collective-permute-start(bf16[288,128]{1,0:T(8,128)(2,1)S(1)} %get-tuple-element.85.own), channel_id=1, source_target_pairs={{0,16},{1,17},{2,18},{3,19},{4,20},{5,21},{6,22},{7,23},{8,24},{9,... | collective-permute-start | bytes 221192 | tf_op jit(solution)/shard_map/ppermute | solution.py:544
  55.5 4.7 %collective-permute-start.12 = (bf16[288,128]{1,0:T(8,128)(2,1)S(1)}, bf16[288,128]{1,0:T(8,128)(2,1)S(1)}, u32[]{:S(2)}, u32[]{:S(2)}) collective-permute-start(bf16[288,128]{1,0:T(8,128)(2,1)S(1)} %get-tuple-element.87.own), channel_id=1, source_target_pairs={{0,48},{1,49},{2,50},{3,51},{4,52},{5,53},{6,54},{7,55},{8,56},{9,... | collective-permute-start | bytes 221192 | tf_op jit(solution)/shard_map/ppermute | solution.py:544
  60.4 3.3 %collective-permute-start.13 = (bf16[288,128]{1,0:T(8,128)(2,1)S(1)}, bf16[288,128]{1,0:T(8,128)(2,1)S(1)}, u32[]{:S(2)}, u32[]{:S(2)}) collective-permute-start(bf16[288,128]{1,0:T(8,128)(2,1)S(1)} %get-tuple-element.89.own), channel_id=1, source_target_pairs={{0,64},{1,65},{2,66},{3,67},{4,68},{5,69},{6,70},{7,71},{8,72},{9,... | collective-permute-start | bytes 221192 | tf_op jit(solution)/shard_map/ppermute | solution.py:544
  64.0 4.5 %collective-permute-start.14 = (bf16[288,128]{1,0:T(8,128)(2,1)S(1)}, bf16[288,128]{1,0:T(8,128)(2,1)S(1)}, u32[]{:S(2)}, u32[]{:S(2)}) collective-permute-start(bf16[288,128]{1,0:T(8,128)(2,1)S(1)} %get-tuple-element.91.own), channel_id=1, source_target_pairs={{0,192},{1,193},{2,194},{3,195},{4,196},{5,197},{6,198},{7,199},{8... | collective-permute-start | bytes 221192 | tf_op jit(solution)/shard_map/ppermute | solution.py:546
  68.5 17.7 %copy-start.1 = (bf16[8,512,256]{2,1,0:T(8,128)(2,1)S(1)}, bf16[8,512,256]{2,1,0:T(8,128)(2,1)}, u32[]{:S(2)}) copy-start(bf16[8,512,256]{2,1,0:T(8,128)(2,1)} %get-tuple-element.78.down) | copy-start | bytes 6291460
  76.9 9.4 %collective-permute-start.15 = (bf16[288,128]{1,0:T(8,128)(2,1)S(1)}, bf16[288,128]{1,0:T(8,128)(2,1)S(1)}, u32[]{:S(2)}, u32[]{:S(2)}) collective-permute-start(bf16[288,128]{1,0:T(8,128)(2,1)S(1)} %get-tuple-element.96.own), channel_id=1, source_target_pairs={{0,1},{1,0},{2,3},{3,2},{4,5},{5,4},{6,7},{7,6},{8,9},{9,8},{10,11... | collective-permute-start | bytes 221192 | tf_op jit(solution)/shard_map/ppermute | solution.py:544
  86.6 4.4 %collective-permute-start.16 = (bf16[288,128]{1,0:T(8,128)(2,1)S(1)}, bf16[288,128]{1,0:T(8,128)(2,1)S(1)}, u32[]{:S(2)}, u32[]{:S(2)}) collective-permute-start(bf16[288,128]{1,0:T(8,128)(2,1)S(1)} %get-tuple-element.97.own), channel_id=1, source_target_pairs={{0,2},{1,3},{2,0},{3,1},{4,6},{5,7},{6,4},{7,5},{8,10},{9,11},{10,... | collective-permute-start | bytes 221192 | tf_op jit(solution)/shard_map/ppermute | solution.py:544
  91.3 5.4 %collective-permute-start.17 = (bf16[288,128]{1,0:T(8,128)(2,1)S(1)}, bf16[288,128]{1,0:T(8,128)(2,1)S(1)}, u32[]{:S(2)}, u32[]{:S(2)}) collective-permute-start(bf16[288,128]{1,0:T(8,128)(2,1)S(1)} %get-tuple-element.99.own), channel_id=1, source_target_pairs={{0,4},{1,5},{2,6},{3,7},{4,0},{5,1},{6,2},{7,3},{8,12},{9,13},{10,... | collective-permute-start | bytes 221192 | tf_op jit(solution)/shard_map/ppermute | solution.py:544
  97.0 5.4 %collective-permute-start.18 = (bf16[288,128]{1,0:T(8,128)(2,1)S(1)}, bf16[288,128]{1,0:T(8,128)(2,1)S(1)}, u32[]{:S(2)}, u32[]{:S(2)}) collective-permute-start(bf16[288,128]{1,0:T(8,128)(2,1)S(1)} %get-tuple-element.101.own), channel_id=1, source_target_pairs={{0,12},{1,13},{2,14},{3,15},{4,8},{5,9},{6,10},{7,11},{8,4},{9,5},... | collective-permute-start | bytes 221192 | tf_op jit(solution)/shard_map/ppermute | solution.py:544
  102.7 3.3 %collective-permute-start.19 = (bf16[288,128]{1,0:T(8,128)(2,1)S(1)}, bf16[288,128]{1,0:T(8,128)(2,1)S(1)}, u32[]{:S(2)}, u32[]{:S(2)}) collective-permute-start(bf16[288,128]{1,0:T(8,128)(2,1)S(1)} %get-tuple-element.103.own), channel_id=1, source_target_pairs={{0,16},{1,17},{2,18},{3,19},{4,20},{5,21},{6,22},{7,23},{8,24},{9,... | collective-permute-start | bytes 221192 | tf_op jit(solution)/shard_map/ppermute | solution.py:544
  106.3 4.5 %collective-permute-start.20 = (bf16[288,128]{1,0:T(8,128)(2,1)S(1)}, bf16[288,128]{1,0:T(8,128)(2,1)S(1)}, u32[]{:S(2)}, u32[]{:S(2)}) collective-permute-start(bf16[288,128]{1,0:T(8,128)(2,1)S(1)} %get-tuple-element.105.own), channel_id=1, source_target_pairs={{0,48},{1,49},{2,50},{3,51},{4,52},{5,53},{6,54},{7,55},{8,56},{9,... | collective-permute-start | bytes 221192 | tf_op jit(solution)/shard_map/ppermute | solution.py:544
  111.1 3.6 %collective-permute-start.21 = (bf16[288,128]{1,0:T(8,128)(2,1)S(1)}, bf16[288,128]{1,0:T(8,128)(2,1)S(1)}, u32[]{:S(2)}, u32[]{:S(2)}) collective-permute-start(bf16[288,128]{1,0:T(8,128)(2,1)S(1)} %get-tuple-element.107.own), channel_id=1, source_target_pairs={{0,64},{1,65},{2,66},{3,67},{4,68},{5,69},{6,70},{7,71},{8,72},{9,... | collective-permute-start | bytes 221192 | tf_op jit(solution)/shard_map/ppermute | solution.py:544
  114.9 4.5 %collective-permute-start.22 = (bf16[288,128]{1,0:T(8,128)(2,1)S(1)}, bf16[288,128]{1,0:T(8,128)(2,1)S(1)}, u32[]{:S(2)}, u32[]{:S(2)}) collective-permute-start(bf16[288,128]{1,0:T(8,128)(2,1)S(1)} %get-tuple-element.109.own), channel_id=1, source_target_pairs={{0,192},{1,193},{2,194},{3,195},{4,196},{5,197},{6,198},{7,199},{8... | collective-permute-start | bytes 221192 | tf_op jit(solution)/shard_map/ppermute | solution.py:546
  127.8 7.6 %collective-permute-start.23 = (bf16[288,128]{1,0:T(8,128)(2,1)S(1)}, bf16[288,128]{1,0:T(8,128)(2,1)S(1)}, u32[]{:S(2)}, u32[]{:S(2)}) collective-permute-start(bf16[288,128]{1,0:T(8,128)(2,1)S(1)} %get-tuple-element.118.own), channel_id=1, source_target_pairs={{0,1},{1,0},{2,3},{3,2},{4,5},{5,4},{6,7},{7,6},{8,9},{9,8},{10,11... | collective-permute-start | bytes 221192 | tf_op jit(solution)/shard_map/ppermute | solution.py:544
  135.7 4.3 %collective-permute-start.24 = (bf16[288,128]{1,0:T(8,128)(2,1)S(1)}, bf16[288,128]{1,0:T(8,128)(2,1)S(1)}, u32[]{:S(2)}, u32[]{:S(2)}) collective-permute-start(bf16[288,128]{1,0:T(8,128)(2,1)S(1)} %get-tuple-element.119.own), channel_id=1, source_target_pairs={{0,2},{1,3},{2,0},{3,1},{4,6},{5,7},{6,4},{7,5},{8,10},{9,11},{10,... | collective-permute-start | bytes 221192 | tf_op jit(solution)/shard_map/ppermute | solution.py:544
  140.4 5.6 %collective-permute-start.25 = (bf16[288,128]{1,0:T(8,128)(2,1)S(1)}, bf16[288,128]{1,0:T(8,128)(2,1)S(1)}, u32[]{:S(2)}, u32[]{:S(2)}) collective-permute-start(bf16[288,128]{1,0:T(8,128)(2,1)S(1)} %get-tuple-element.121.own), channel_id=1, source_target_pairs={{0,4},{1,5},{2,6},{3,7},{4,0},{5,1},{6,2},{7,3},{8,12},{9,13},{10,... | collective-permute-start | bytes 221192 | tf_op jit(solution)/shard_map/ppermute | solution.py:544
  146.2 5.4 %collective-permute-start.26 = (bf16[288,128]{1,0:T(8,128)(2,1)S(1)}, bf16[288,128]{1,0:T(8,128)(2,1)S(1)}, u32[]{:S(2)}, u32[]{:S(2)}) collective-permute-start(bf16[288,128]{1,0:T(8,128)(2,1)S(1)} %get-tuple-element.123.own), channel_id=1, source_target_pairs={{0,12},{1,13},{2,14},{3,15},{4,8},{5,9},{6,10},{7,11},{8,4},{9,5},... | collective-permute-start | bytes 221192 | tf_op jit(solution)/shard_map/ppermute | solution.py:544
  151.9 3.3 %collective-permute-start.27 = (bf16[288,128]{1,0:T(8,128)(2,1)S(1)}, bf16[288,128]{1,0:T(8,128)(2,1)S(1)}, u32[]{:S(2)}, u32[]{:S(2)}) collective-permute-start(bf16[288,128]{1,0:T(8,128)(2,1)S(1)} %get-tuple-element.125.own), channel_id=1, source_target_pairs={{0,16},{1,17},{2,18},{3,19},{4,20},{5,21},{6,22},{7,23},{8,24},{9,... | collective-permute-start | bytes 221192 | tf_op jit(solution)/shard_map/ppermute | solution.py:544
  155.5 4.5 %collective-permute-start.28 = (bf16[288,128]{1,0:T(8,128)(2,1)S(1)}, bf16[288,128]{1,0:T(8,128)(2,1)S(1)}, u32[]{:S(2)}, u32[]{:S(2)}) collective-permute-start(bf16[288,128]{1,0:T(8,128)(2,1)S(1)} %get-tuple-element.127.own), channel_id=1, source_target_pairs={{0,48},{1,49},{2,50},{3,51},{4,52},{5,53},{6,54},{7,55},{8,56},{9,... | collective-permute-start | bytes 221192 | tf_op jit(solution)/shard_map/ppermute | solution.py:544
  160.3 3.6 %collective-permute-start.29 = (bf16[288,128]{1,0:T(8,128)(2,1)S(1)}, bf16[288,128]{1,0:T(8,128)(2,1)S(1)}, u32[]{:S(2)}, u32[]{:S(2)}) collective-permute-start(bf16[288,128]{1,0:T(8,128)(2,1)S(1)} %get-tuple-element.129.own), channel_id=1, source_target_pairs={{0,64},{1,65},{2,66},{3,67},{4,68},{5,69},{6,70},{7,71},{8,72},{9,... | collective-permute-start | bytes 221192 | tf_op jit(solution)/shard_map/ppermute | solution.py:544
  164.2 4.5 %collective-permute-start.30 = (bf16[288,128]{1,0:T(8,128)(2,1)S(1)}, bf16[288,128]{1,0:T(8,128)(2,1)S(1)}, u32[]{:S(2)}, u32[]{:S(2)}) collective-permute-start(bf16[288,128]{1,0:T(8,128)(2,1)S(1)} %get-tuple-element.131.own), channel_id=1, source_target_pairs={{0,192},{1,193},{2,194},{3,195},{4,196},{5,197},{6,198},{7,199},{8... | collective-permute-start | bytes 221192 | tf_op jit(solution)/shard_map/ppermute | solution.py:546
  (20 other events, 178.5 us)
